TPU v7x, 32 devices: a whole 2x2x4 slice. The times are simulated.
32 devices in a mesh: dp: 8 (over y, x, core), blk: 4 (over z).
Axes of the slice: x: 2, y: 2, z: 4, core: 2. Of those that a mesh axis runs over, the one named last changes fastest.
Arguments:
- token_ids: int32 [16384], P(('dp', 'blk')), may hold values from 0 to 831
- segment_ids: int32 [16384], P(('dp', 'blk')), may hold values from 0 to 3, as said below
- timesteps: int32 [16384], P(('dp', 'blk')), may hold values from 0 to 1999, as said below
- noise: float32 [16384, 16], P(('dp', 'blk')), may hold values from -6 to 6
- table: float32 [832, 16], P('dp')
- up_weight: bfloat16 [16, 768], replicated, may hold values from -1.5 to 1.5
- up_bias: float32 [768], replicated, may hold values from -1.75 to 1.75
- norm1_gain: float32 [768], replicated, may hold values from 0.5 to 1.5
- norm1_shift: float32 [768], replicated, may hold values from -1.75 to 1.75
- qkv_weight: bfloat16 [768, 2304], replicated, may hold values from -0.21875 to 0.21875
- query_bias: float32 [768], replicated, may hold values from -1.75 to 1.75
- value_bias: float32 [768], replicated, may hold values from -1.75 to 1.75
- out_weight: bfloat16 [768, 768], replicated, may hold values from -0.875 to 0.875
- out_bias: float32 [768], replicated, may hold values from -1.75 to 1.75
- norm2_gain: float32 [768], replicated, may hold values from 0.5 to 1.5
- norm2_shift: float32 [768], replicated, may hold values from -1.75 to 1.75
- ffn_in_weight: bfloat16 [768, 3072], replicated, may hold values from -0.21875 to 0.21875
- ffn_in_bias: float32 [3072], replicated, may hold values from -1.75 to 1.75
- ffn_out_weight: bfloat16 [3072, 768], replicated, may hold values from -0.109375 to 0.109375
- ffn_out_bias: float32 [768], replicated, may hold values from -1.75 to 1.75
- cotangent: float32 [16384, 768], P(('dp', 'blk')), may hold values from -6 to 6
Outputs:
- block_out: float32 [16384, 768], P(('dp', 'blk'))
- noise_grad: float32 [16384, 16], P(('dp', 'blk'))
- table_grad: float32 [832, 16], P('dp')
- up_weight_grad: float32 [16, 768], replicated
- up_bias_grad: float32 [768], replicated
- norm1_gain_grad: float32 [768], replicated
- norm1_shift_grad: float32 [768], replicated
- qkv_weight_grad: float32 [768, 2304], P(('dp', 'blk'))
- query_bias_grad: float32 [768], replicated
- value_bias_grad: float32 [768], replicated
- out_weight_grad: float32 [768, 768], P(('dp', 'blk'))
- out_bias_grad: float32 [768], replicated
- norm2_gain_grad: float32 [768], replicated
- norm2_shift_grad: float32 [768], replicated
- ffn_in_weight_grad: float32 [768, 3072], P(('dp', 'blk'))
- ffn_in_bias_grad: float32 [3072], replicated
- ffn_out_weight_grad: float32 [3072, 768], P(('dp', 'blk'))
- ffn_out_bias_grad: float32 [768], replicated
- mean_norm: float32 [], replicated
Inputs may be any that keep to these rules, and one draw needn't show every extreme that they name: `segment_ids`: documents are numbered from 0 within each group of 2048 tokens (one index of dp) and lie end to end in the group's order, one to four of them a group, each a multiple of 64 tokens long. `timesteps`: equal for all tokens of one document.
All inputs are finite; a program needn't handle non-finite values.
Results may differ from a plain program's by a relative error of at most 0.017.
Values may be sent and summed in bfloat16 or wider, within the bound.
A program may use at most 192 MiB of HBM per device.

v0:
```python
import math

import jax
import jax.numpy as jnp
from jax import lax
from jax.sharding import PartitionSpec as P

D = 768
HEADS = 12
HEAD_DIM = 64
VOCAB = 832
TSTEPS = 2000


highest = lax.Precision.HIGHEST


def layer_norm(inputs, norm_gain, norm_shift):
    center = jnp.mean(inputs, axis=-1, keepdims=True)
    centered = inputs - center
    spread = jnp.mean(centered * centered, axis=-1, keepdims=True)
    return centered * lax.rsqrt(spread + 1e-05) * norm_gain + norm_shift


def sinusoid(steps_float, width):
    half_width = width // 2
    frequency = jnp.exp(-math.log(10000.0) * jnp.arange(half_width, dtype=jnp.float32) / half_width)
    angles = steps_float[:, None] * frequency[None, :]
    return jnp.concatenate([jnp.sin(angles), jnp.cos(angles)], axis=-1)


def matmul(left, right):
    return jnp.dot(left, right, preferred_element_type=jnp.float32)


def over_rows(left, right):
    return lax.dot_general(
        left, right, (((0,), (0,)), ((), ())), preferred_element_type=jnp.float32
    )


def against(left, right):
    return lax.dot_general(
        left, right, (((1,), (1,)), ((), ())), preferred_element_type=jnp.float32
    )


def key_blocks(key_rows, value_rows, key_segments):
    count = key_rows.shape[0]
    block_size = math.gcd(count, 512)
    blocks = count // block_size
    return (
        key_rows.reshape(blocks, block_size, HEADS, HEAD_DIM),
        value_rows.reshape(blocks, block_size, HEADS, HEAD_DIM),
        key_segments.reshape(blocks, block_size),
    )


def attend_forward(state, query_heads, query_segments, key_rows, value_rows, key_segments):
    score_scale = HEAD_DIM ** (-0.5)

    def visit(carry, block):
        running_max, running_sum, running_acc = carry
        key_part, value_part, segment_part = block
        scores = (
            jnp.einsum("rhd,khd->rhk", query_heads, key_part, preferred_element_type=jnp.float32)
            * score_scale
        )
        allowed = query_segments[:, None, None] == segment_part[None, None, :]
        scores = jnp.where(allowed, scores, -1e30)
        new_max = jnp.maximum(running_max, jnp.max(scores, axis=-1))
        ratio = jnp.exp(running_max - new_max)
        weights = jnp.where(allowed, jnp.exp(scores - new_max[..., None]), 0.0)
        running_sum = running_sum * ratio + jnp.sum(weights, axis=-1)
        running_acc = running_acc * ratio[..., None] + jnp.einsum(
            "rhk,khd->rhd",
            weights.astype(jnp.bfloat16),
            value_part,
            preferred_element_type=jnp.float32,
        )
        return ((new_max, running_sum, running_acc), None)

    state, unused = lax.scan(visit, state, key_blocks(key_rows, value_rows, key_segments))
    return state


def attend_backward(
    query_heads, query_segments, grad_heads, log_total, delta, key_rows, value_rows, key_segments
):
    score_scale = HEAD_DIM ** (-0.5)
    local_rows = query_heads.shape[0]

    def visit(query_grad, block):
        key_part, value_part, segment_part = block
        scores = (
            jnp.einsum("rhd,khd->rhk", query_heads, key_part, preferred_element_type=jnp.float32)
            * score_scale
        )
        allowed = query_segments[:, None, None] == segment_part[None, None, :]
        probs = jnp.where(allowed, jnp.exp(scores - log_total[..., None]), 0.0)
        prob_grad = jnp.einsum(
            "rhd,khd->rhk", grad_heads, value_part, preferred_element_type=jnp.float32
        )
        score_grad = (probs * (prob_grad - delta[..., None])).astype(jnp.bfloat16)
        joined = None
        query_grad = (
            query_grad
            + jnp.einsum("rhk,khd->rhd", score_grad, key_part, preferred_element_type=jnp.float32)
            * score_scale
        )
        value_grad = jnp.einsum(
            "rhk,rhd->khd",
            probs.astype(jnp.bfloat16),
            grad_heads,
            preferred_element_type=jnp.float32,
        )
        key_grad = (
            jnp.einsum("rhk,rhd->khd", score_grad, query_heads, preferred_element_type=jnp.float32)
            * score_scale
        )
        block_size = key_part.shape[0]
        joined = jnp.concatenate(
            [key_grad.reshape(block_size, D), value_grad.reshape(block_size, D)], axis=1
        )
        return (query_grad, joined)

    start_grad = jnp.zeros((local_rows, HEADS, HEAD_DIM), jnp.float32)
    query_grad, joined = lax.scan(visit, start_grad, key_blocks(key_rows, value_rows, key_segments))
    key_result = joined.reshape(key_rows.shape[0], 2 * D)
    return (key_result, query_grad.reshape(local_rows, D))


def shards(
    token_ids,
    segment_ids,
    timesteps,
    noise,
    table,
    up_weight,
    up_bias,
    norm1_gain,
    norm1_shift,
    qkv_weight,
    query_bias,
    value_bias,
    out_weight,
    out_bias,
    norm2_gain,
    norm2_shift,
    ffn_in_weight,
    ffn_in_bias,
    ffn_out_weight,
    ffn_out_bias,
    cotangent,
):
    local_rows = token_ids.shape[0]
    full_table = lax.all_gather(table, "dp", axis=0, tiled=True)
    local_norms = jnp.sqrt(jnp.sum(table * table, axis=-1) + 1.0)
    mean_norm = lax.psum(jnp.sum(local_norms), "dp") / VOCAB
    vocab_index = lax.broadcasted_iota(jnp.int32, (local_rows, VOCAB), 1)
    one_hot = (token_ids[:, None] == vocab_index).astype(jnp.float32)
    picked = jnp.dot(one_hot, full_table, precision=highest, preferred_element_type=jnp.float32)
    embedded = picked / mean_norm
    steps_float = timesteps.astype(jnp.float32)
    alpha_bar = 1.0 - jnp.sqrt(steps_float / TSTEPS + 0.0001)
    signal_scale = jnp.sqrt(alpha_bar)[:, None]
    noise_scale = jnp.sqrt(1.0 - alpha_bar)[:, None]
    mixed = (signal_scale * embedded + noise_scale * noise).astype(jnp.bfloat16)
    hidden0 = matmul(mixed, up_weight) + up_bias + sinusoid(steps_float, D)
    first_norm, first_pull = jax.vjp(layer_norm, hidden0, norm1_gain, norm1_shift)
    normed = first_norm.astype(jnp.bfloat16)
    bias_row = jnp.concatenate([query_bias, jnp.zeros((D,), jnp.float32), value_bias])
    qkv = (matmul(normed, qkv_weight) + bias_row).astype(jnp.bfloat16)
    queries = qkv[:, :D]
    keys = qkv[:, D : 2 * D]
    values = qkv[:, 2 * D :]
    query_heads = queries.reshape(local_rows, HEADS, HEAD_DIM)
    segment_all = lax.all_gather(segment_ids, "blk", axis=0, tiled=True)
    initial = (
        jnp.full((local_rows, HEADS), -1e30, jnp.float32),
        jnp.zeros((local_rows, HEADS), jnp.float32),
        jnp.zeros((local_rows, HEADS, HEAD_DIM), jnp.float32),
    )
    key_rows = lax.all_gather(keys, "blk", axis=0, tiled=True)
    value_rows = lax.all_gather(values, "blk", axis=0, tiled=True)
    state = attend_forward(initial, query_heads, segment_ids, key_rows, value_rows, segment_all)
    running_max, running_sum, running_acc = state
    attended_heads = running_acc / running_sum[..., None]
    log_total = running_max + jnp.log(running_sum)
    attended = attended_heads.reshape(local_rows, D).astype(jnp.bfloat16)
    hidden1 = hidden0 + matmul(attended, out_weight) + out_bias
    second_norm, second_pull = jax.vjp(layer_norm, hidden1, norm2_gain, norm2_shift)
    normed2 = second_norm.astype(jnp.bfloat16)
    inner = matmul(normed2, ffn_in_weight) + ffn_in_bias
    activated, gelu_pull = jax.vjp(jax.nn.gelu, inner)
    active = activated.astype(jnp.bfloat16)
    block_out = hidden1 + matmul(active, ffn_out_weight) + ffn_out_bias
    out_grad = cotangent.astype(jnp.bfloat16)
    outer_weight_term = over_rows(active, out_grad)
    outer_bias_term = jnp.sum(out_grad, axis=0, dtype=jnp.float32)
    inner_grad = gelu_pull(against(out_grad, ffn_out_weight))[0].astype(jnp.bfloat16)
    inner_weight_term = over_rows(normed2, inner_grad)
    inner_bias_term = jnp.sum(inner_grad, axis=0, dtype=jnp.float32)
    hidden1_part, gain_two_term, shift_two_term = second_pull(against(inner_grad, ffn_in_weight))
    hidden1_grad = cotangent + hidden1_part
    branch_grad = hidden1_grad.astype(jnp.bfloat16)
    out_weight_term = over_rows(attended, branch_grad)
    out_bias_term = jnp.sum(branch_grad, axis=0, dtype=jnp.float32)
    attended_grad = against(branch_grad, out_weight).astype(jnp.bfloat16)
    grad_heads = attended_grad.reshape(local_rows, HEADS, HEAD_DIM)
    delta = jnp.sum(grad_heads.astype(jnp.float32) * attended_heads, axis=-1)
    key_back, value_back = (
        lax.all_gather(keys, "blk", axis=0, tiled=True),
        lax.all_gather(values, "blk", axis=0, tiled=True),
    )
    kv_terms, query_grad = attend_backward(
        query_heads, segment_ids, grad_heads, log_total, delta, key_back, value_back, segment_all
    )
    kv_mine = lax.psum_scatter(
        kv_terms.astype(jnp.bfloat16), "blk", scatter_dimension=0, tiled=True
    ).astype(jnp.float32)
    qkv_grad = jnp.concatenate([query_grad, kv_mine], axis=1).astype(jnp.bfloat16)
    qkv_weight_term = over_rows(normed, qkv_grad)
    query_bias_term = jnp.sum(qkv_grad[:, :D], axis=0, dtype=jnp.float32)
    value_bias_term = jnp.sum(qkv_grad[:, 2 * D :], axis=0, dtype=jnp.float32)
    hidden0_part, gain_one_term, shift_one_term = first_pull(against(qkv_grad, qkv_weight))
    hidden0_grad = (hidden1_grad + hidden0_part).astype(jnp.bfloat16)
    up_weight_term = over_rows(mixed, hidden0_grad)
    up_bias_term = jnp.sum(hidden0_grad, axis=0, dtype=jnp.float32)
    mixed_grad = against(hidden0_grad, up_weight)
    noise_grad = noise_scale * mixed_grad
    embedded_grad = signal_scale * mixed_grad
    table_term = lax.dot_general(
        one_hot,
        embedded_grad / mean_norm,
        (((0,), (0,)), ((), ())),
        precision=highest,
        preferred_element_type=jnp.float32,
    )
    norm_term = -jnp.sum(embedded_grad * picked) / (mean_norm * mean_norm)
    (
        up_weight_grad,
        up_bias_grad,
        norm1_gain_grad,
        norm1_shift_grad,
        query_bias_grad,
        value_bias_grad,
        out_bias_grad,
        norm2_gain_grad,
        norm2_shift_grad,
        ffn_in_bias_grad,
        ffn_out_bias_grad,
        norm_grad,
        table_total,
    ) = lax.psum(
        (
            up_weight_term,
            up_bias_term,
            gain_one_term,
            shift_one_term,
            query_bias_term,
            value_bias_term,
            out_bias_term,
            gain_two_term,
            shift_two_term,
            inner_bias_term,
            outer_bias_term,
            norm_term,
            table_term,
        ),
        ("dp", "blk"),
    )
    qkv_weight_grad, out_weight_grad, ffn_in_weight_grad, ffn_out_weight_grad = (
        lax.psum_scatter(qkv_weight_term, ("dp", "blk"), scatter_dimension=0, tiled=True),
        lax.psum_scatter(out_weight_term, ("dp", "blk"), scatter_dimension=0, tiled=True),
        lax.psum_scatter(inner_weight_term, ("dp", "blk"), scatter_dimension=0, tiled=True),
        lax.psum_scatter(outer_weight_term, ("dp", "blk"), scatter_dimension=0, tiled=True),
    )
    row_start = lax.axis_index("dp") * table.shape[0]
    table_grad = lax.dynamic_slice_in_dim(table_total, row_start, table.shape[0], 0)
    table_grad = table_grad + norm_grad * table / (VOCAB * local_norms[:, None])
    return (
        block_out,
        noise_grad,
        table_grad,
        up_weight_grad,
        up_bias_grad,
        norm1_gain_grad,
        norm1_shift_grad,
        qkv_weight_grad,
        query_bias_grad,
        value_bias_grad,
        out_weight_grad,
        out_bias_grad,
        norm2_gain_grad,
        norm2_shift_grad,
        ffn_in_weight_grad,
        ffn_in_bias_grad,
        ffn_out_weight_grad,
        ffn_out_bias_grad,
        mean_norm,
    )


def solution(mesh):
    in_specs = (
        P(("dp", "blk")),
        P(("dp", "blk")),
        P(("dp", "blk")),
        P(("dp", "blk"), None),
        P("dp", None),
        P(),
        P(),
        P(),
        P(),
        P(),
        P(),
        P(),
        P(),
        P(),
        P(),
        P(),
        P(),
        P(),
        P(),
        P(),
        P(("dp", "blk"), None),
    )
    out_specs = (
        P(("dp", "blk"), None),
        P(("dp", "blk"), None),
        P("dp", None),
        P(),
        P(),
        P(),
        P(),
        P(("dp", "blk"), None),
        P(),
        P(),
        P(("dp", "blk"), None),
        P(),
        P(),
        P(),
        P(("dp", "blk"), None),
        P(),
        P(("dp", "blk"), None),
        P(),
        P(),
    )
    return jax.shard_map(shards, mesh=mesh, in_specs=in_specs, out_specs=out_specs, check_vma=False)
```

profile of v0, /device:TPU:0, one launch (start us, length us, event | category | flops | bytes accessed | tf_op | source)
XLA Modules:
  0.0 1041.3 jit_solution(15761555475671102674)
XLA Ops:
  10.8 15.8 %psum.98 = f32[]{:T(128)} all-reduce(f32[]{:T(128)} %get-tuple-element.361), channel_id=1, replica_groups=mesh['dp'=8,'blk'=4] {'dp'}, use_global_device_ids=true, to_apply=%region_2.0 | all-reduce | flops 1 | bytes 8 | tf_op jit(solution)/shard_map/psum | solution.py:159
  26.6 8.4 all-gather
  50.0 12.7 %all-gather.1 = s32[4,1,512]{2,1,0:T(1,128)S(1)} all-gather(s32[1,1,512]{2,1,0:T(1,128)S(1)} %bitcast.164), channel_id=1, replica_groups=mesh['dp'=8,'blk'=4] {'blk'}, dimensions={0}, use_global_device_ids=true | all-gather | bytes 10240 | tf_op jit(solution)/shard_map/all_gather | solution.py:178
  65.1 48.0 %all-gather.7.cloned.1.call-done = bf16[2048,768]{1,0:T(8,128)(2,1)} async-done(((bf16[512,768]{1,0:T(8,128)(2,1)}), bf16[2048,768]{1,0:T(8,128)(2,1)}) %all-gather.7.cloned.1.call-update) | async-done | bytes 3145744 | tf_op jit(solution)/shard_map/all_gather | solution.py:185
  113.1 4.7 copy.90
  117.8 6.3 reshape.224
  124.1 4.3 copy.92
  128.4 48.5 %all-gather.5.cloned.1.call-done = bf16[2048,768]{1,0:T(8,128)(2,1)} async-done(((bf16[512,768]{1,0:T(8,128)(2,1)}), bf16[2048,768]{1,0:T(8,128)(2,1)}) %all-gather.5.cloned.1.call-update) | async-done | bytes 3145744 | tf_op jit(solution)/shard_map/all_gather | solution.py:184
  176.8 4.8 copy.88
  181.6 6.2 reshape.222
  187.8 4.3 copy.91
  192.0 51.3 %while.28 = (s32[]{:T(128)}, f32[512,12]{0,1:T(8,128)}, f32[512,12]{0,1:T(8,128)}, f32[512,12,64]{0,2,1:T(8,128)}, s32[512]{0:T(512)S(1)}, /*index=5*/s32[4,512]...) while((s32[]{:T(128)}, f32[512,12]{0,1:T(8,128)}, ...), condition=%wide.region_8.9_spmd.clone, body=%wide.region_5.8_spmd.clone.sunk | while | flops 847673344 | bytes 57581848 | solution.py:83
  192.3 3.4 fusion.131
  195.8 3.1 fusion.132
  199.0 4.7 bitcast_add_fusion.4
  205.1 3.4 fusion.131
  211.8 4.7 bitcast_add_fusion.4
  218.0 3.4 fusion.131
  224.7 4.7 bitcast_add_fusion.4
  230.8 3.4 fusion.131
  237.5 4.7 bitcast_add_fusion.4
  249.5 4.9 fusion.72
  254.5 7.3 convert_reduce_fusion
  261.9 3.5 multiply_reduce_fusion
  275.5 134.3 %while.29 = (s32[]{:T(128)}, f32[512,12,64]{0,2,1:T(8,128)}, bf16[4,512,1536]{2,1,0:T(8,128)(2,1)}, bf16[4,512,12,64]{1,3,2,0:T(8,128)(2,1)}, s32[512]{0:T(512)S...) while((s32[]{:T(128)}, f32[512,12,64]{0,2,1:T(8,128)}, ...), condition=%wide.region_15.16_spmd.clone, body=%wide.region_14.15_spmd.clone.sunk | while | flops 2050097152 | bytes 96223568 | solution.py:128
  276.0 7.8 fusion.144
  283.8 6.1 fusion.146
  289.9 7.3 fusion.145
  309.5 7.8 fusion.144
  317.3 6.1 fusion.146
  323.4 7.3 fusion.145
  343.0 7.8 fusion.144
  350.8 6.1 fusion.146
  356.9 7.3 fusion.145
  376.5 7.8 fusion.144
  384.3 6.1 fusion.146
  390.4 7.3 fusion.145
  409.9 3.6 fusion.80
  413.6 11.8 %fusion.65 = f32[3072,768]{1,0:T(8,128)} fusion(f32[512,768]{1,0:T(8,128)} %param.45, f32[512,3072]{1,0:T(8,128)} %copy-done.60, f32[3072]{0:T(1024)S(1)} %copy-done.55), kind=kOutput, calls=%fused_computation.131 | convolution fusion | flops 2432040960 | bytes 17313792 | tf_op jit(solution)/shard_map/dot_general | solution.py:37
  426.1 9.0 fusion.71
  440.5 78.9 %reduce-scatter.6.cloned.1.call-done = bf16[512,1536]{1,0:T(8,128)(2,1)} async-done(((bf16[2048,1536]{1,0:T(8,128)(2,1)}), bf16[512,1536]{1,0:T(8,128)(2,1)}) %reduce-scatter.6.cloned.1.call-update) | async-done | bytes 1572880 | tf_op jit(solution)/shard_map/reduce_scatter | solution.py:219
  519.4 7.2 fusion.49
  527.9 9.9 add_add_fusion.3
  552.8 45.1 %all-reduce.2 = (f32[832,16]{0,1:T(8,128)}, f32[]{:T(128)}, f32[16,768]{1,0:T(8,128)}, f32[768]{0:T(1024)}, f32[768]{0:T(1024)}, /*index=5*/f32[768]{0:T(1024)},...) all-reduce(f32[832,16]{0,1:T(8,128)} %fusion.47, ...), channel_id=1, replica_groups=mesh['dp'=8,'blk'=4] {'dp','blk'}, use_global_device_ids=true, to_apply=%region_19.20 | all-reduce | flops 35585 | bytes 284680 | tf_op jit(solution)/shard_map/psum | solution.py:255
  599.9 24.7 %reduce-scatter.10.cloned.1.call-done = f32[24,768]{1,0:T(8,128)} async-done(((f32[768,768]{1,0:T(8,128)}), f32[24,768]{1,0:T(8,128)}) %reduce-scatter.10.cloned.1.call-update) | async-done | bytes 73744 | tf_op jit(solution)/shard_map/reduce_scatter | solution.py:275
  624.6 142.0 %reduce-scatter.14.cloned.1.call-done = f32[96,768]{1,0:T(8,128)} async-done(((f32[3072,768]{1,0:T(8,128)}), f32[96,768]{1,0:T(8,128)}) %reduce-scatter.14.cloned.1.call-update) | async-done | bytes 294928 | tf_op jit(solution)/shard_map/reduce_scatter | solution.py:277
  766.6 141.0 %reduce-scatter.12.cloned.1.call-done = f32[24,3072]{1,0:T(8,128)} async-done(((f32[768,3072]{1,0:T(8,128)}), f32[24,3072]{1,0:T(8,128)}) %reduce-scatter.12.cloned.1.call-update) | async-done | bytes 294928 | tf_op jit(solution)/shard_map/reduce_scatter | solution.py:276
  907.6 125.2 %reduce-scatter.8.cloned.1.call-done = f32[24,2304]{1,0:T(8,128)} async-done(((f32[768,2304]{1,0:T(8,128)}), f32[24,2304]{1,0:T(8,128)}) %reduce-scatter.8.cloned.1.call-update) | async-done | bytes 221200 | tf_op jit(solution)/shard_map/reduce_scatter | solution.py:274
  (314 shorter events, 122.8 us)
Async XLA Ops:
  7.2 38.3 %copy-start = (bf16[768,2304]{1,0:T(8,128)(2,1)S(1)}, bf16[768,2304]{1,0:T(8,128)(2,1)}, u32[]{:S(2)}) copy-start(bf16[768,2304]{1,0:T(8,128)(2,1)} %param.34) | copy-start | bytes 10616836
  7.2 105.9 %all-gather.7.cloned.1.call-start = ((), (), s32[]{:S(2)}) async-start(), calls=%async_computation.6 | async-start | bytes 3932160 | tf_op jit(solution)/shard_map/all_gather | solution.py:185
  9.0 35.3 %copy-start.43 = (f32[512]{0:T(512)}, f32[512]{0:T(512)S(1)}, u32[]{:S(2)}) copy-start(f32[512]{0:T(512)S(1)} %get-tuple-element.358) | copy-start | bytes 6148
  9.0 35.3 %copy-start.45 = (f32[512]{0:T(512)}, f32[512]{0:T(512)S(1)}, u32[]{:S(2)}) copy-start(f32[512]{0:T(512)S(1)} %get-tuple-element.359) | copy-start | bytes 6148
  49.1 127.7 %all-gather.5.cloned.1.call-start = ((), (), s32[]{:S(2)}) async-start(), calls=%async_computation.5 | async-start | bytes 3932160 | tf_op jit(solution)/shard_map/all_gather | solution.py:184
  49.9 469.5 %reduce-scatter.6.cloned.1.call-start = ((), (), s32[]{:S(2)}) async-start(), calls=%async_computation.7 | async-start | bytes 7864320 | tf_op jit(solution)/shard_map/reduce_scatter | solution.py:219
  199.0 4.7 copy-start.22
  211.8 4.7 copy-start.22
  224.6 4.7 copy-start.22
  237.5 4.7 copy-start.22
  246.6 7.9 slice-start.2
  249.1 16.3 %copy-start.14 = (f32[512,768]{1,0:T(8,128)}, f32[512,768]{1,0:T(8,128)S(1)}, u32[]{:S(2)}) copy-start(f32[512,768]{1,0:T(8,128)S(1)} %get-tuple-element.367) | copy-start | bytes 4718596
  249.4 16.0 %copy-start.47 = (f32[512]{0:T(512)}, f32[512]{0:T(512)S(1)}, u32[]{:S(2)}) copy-start(f32[512]{0:T(512)S(1)} %fusion.60) | copy-start | bytes 6148
  249.5 5.0 copy-start.12
  249.5 5.0 slice-start.3
  249.5 5.0 copy-start.54
  249.5 12.3 %slice-start = ((s8[4718592]{0:T(1024)(128)(4,1)}), s8[4194304]{0:T(1024)(128)(4,1)S(1)}, s32[]{:S(2)}) async-start(s8[4718592]{0:T(1024)(128)(4,1)} %bitcast.169), calls=%async_computation.12 | async-start | bytes 8388608
  254.5 7.3 copy-start.60
  254.5 7.3 slice-start.1
  275.9 7.8 copy-start.18
  276.0 7.8 copy-start.37
  283.8 6.1 copy-start.35
  289.9 7.3 copy-start.1
  309.5 7.8 copy-start.18
  309.5 7.8 copy-start.37
  317.3 6.1 copy-start.35
  323.4 7.3 copy-start.1
  343.0 7.8 copy-start.18
  343.0 7.8 copy-start.37
  350.8 6.1 copy-start.35
  356.9 7.3 copy-start.1
  376.5 7.8 copy-start.18
  376.5 7.8 copy-start.37
  384.3 6.1 copy-start.35
  390.4 7.3 copy-start.1
  409.9 214.8 %reduce-scatter.10.cloned.1.call-start = ((), (), s32[]{:S(2)}) async-start(), calls=%async_computation.9 | async-start | bytes 2433024 | tf_op jit(solution)/shard_map/reduce_scatter | solution.py:275
  413.6 353.1 %reduce-scatter.14.cloned.1.call-start = ((), (), s32[]{:S(2)}) async-start(), calls=%async_computation.11 | async-start | bytes 9732096 | tf_op jit(solution)/shard_map/reduce_scatter | solution.py:277
  425.4 482.2 %reduce-scatter.12.cloned.1.call-start = ((), (), s32[]{:S(2)}) async-start(), calls=%async_computation.10 | async-start | bytes 9732096 | tf_op jit(solution)/shard_map/reduce_scatter | solution.py:276
  435.1 84.3 %copy-start.25 = (f32[768]{0:T(1024)S(1)}, f32[768]{0:T(1024)}, u32[]{:S(2)}) copy-start(f32[768]{0:T(1024)} %param.32) | copy-start | bytes 9220
  435.2 84.3 %copy-start.27 = (f32[512]{0:T(512)S(1)}, f32[512]{0:T(512)}, u32[]{:S(2)}) copy-start(f32[512]{0:T(512)} %copy-done.26) | copy-start | bytes 6148
  435.2 84.3 %copy-start.29 = (f32[768]{0:T(1024)S(1)}, f32[768]{0:T(1024)}, u32[]{:S(2)}) copy-start(f32[768]{0:T(1024)} %param.33) | copy-start | bytes 9220
  435.2 84.2 %copy-start.31 = (f32[512]{0:T(512)S(1)}, f32[512]{0:T(512)}, u32[]{:S(2)}) copy-start(f32[512]{0:T(512)} %copy-done.30) | copy-start | bytes 6148
  435.2 597.7 %reduce-scatter.8.cloned.1.call-start = ((), (), s32[]{:S(2)}) async-start(), calls=%async_computation.8 | async-start | bytes 7299072 | tf_op jit(solution)/shard_map/reduce_scatter | solution.py:274
  527.9 9.9 copy-start.6
  527.9 9.9 copy-start.16
  527.9 9.9 copy-start.17
  543.7 9.1 copy-start.42
  543.7 54.2 %copy-start.33 = (f32[104,16]{0,1:T(8,128)S(1)}, f32[104,16]{0,1:T(8,128)}, u32[]{:S(2)}) copy-start(f32[104,16]{0,1:T(8,128)} %param.29) | copy-start | bytes 19972
  (58 other events, 129.8 us)
Sparse Core Ops, SparseCore 0:
  49.3 63.8 all-gather.6
  114.7 62.1 all-gather.4
  410.0 109.3 reduce-scatter.5
  525.1 99.4 reduce-scatter.9
  632.0 134.6 reduce-scatter.13
  773.0 134.6 reduce-scatter.11
  914.8 117.9 reduce-scatter.7
where the time goes:
time: 1050 us; the launch traced here: 1040 us
  waiting for transfers between devices  609 us (58%)
  matrix products  210 us (20%)
  blocking collectives  81.9 us (8%)
  local copies, waits for them, and re-layouts  77.3 us (7%)
  other arithmetic  42.1 us (4%)
  between operations  18.9 us (2%)
    reduce_scatter x1, waiting for transfers between devices, shards(): lax.psum_scatter(outer_weight_term, ('dp', 'blk'), scatter_dimension=0, t...  142 us
    reduce_scatter x1, waiting for transfers between devices, shards(): lax.psum_scatter(inner_weight_term, ('dp', 'blk'), scatter_dimension=0, t...  141 us
    reduce_scatter x1, waiting for transfers between devices, shards(): lax.psum_scatter(qkv_weight_term, ('dp', 'blk'), scatter_dimension=0, til...  125 us
    reduce_scatter x1, waiting for transfers between devices, shards(): lax.psum_scatter(kv_terms.astype(jnp.bfloat16), 'blk', scatter_dimension=...  78.9 us
    all_gather x1, waiting for transfers between devices, shards(): key_rows = lax.all_gather(keys, 'blk', axis=0, tiled=True)  48.5 us
    all_gather x1, waiting for transfers between devices, shards(): value_rows = lax.all_gather(values, 'blk', axis=0, tiled=True)  48 us
    psum x1, blocking collectives, shards(): lax.psum((up_weight_term, up_bias_term, gain_one_term, shift_one_term, qu...  45.1 us
    dot_general x8, matrix products, visit(): jnp.einsum('rhd,khd->rhk', query_heads, key_part, preferred_element_type=...  45 us
  transfers between devices with their start and end apart: 7, of which 7 were waited for; matrix products, arithmetic and copies ran while one was open for 8% of the time, Pallas kernels for 0%

commit v1 on v0

v1 whole, which is shorter than its diff:
```python
import functools
import math

import jax
import jax.numpy as jnp
from jax import lax
from jax.experimental import pallas as pl
from jax.experimental.pallas import tpu as pltpu
from jax.sharding import PartitionSpec as P

D = 768
HEADS = 12
HEAD_DIM = 64
FF = 3072
EMB = 16
TSTEPS = 2000
DOCS = 4
PAIR = 2 * HEAD_DIM
SLOT = 256
EXT = 192
BIG = 1e30
SCALE = HEAD_DIM**-0.5
MIB = 2**20
MESH = pl.DeviceIdType.MESH
VMEM = pltpu.VMEM
f32 = jnp.float32
bf16 = jnp.bfloat16

NN = (((1,), (0,)), ((), ()))
NT = (((1,), (1,)), ((), ()))
TN = (((0,), (0,)), ((), ()))
TT = (((0,), (1,)), ((), ()))


def dot(left, right, dims=NN):
    return lax.dot_general(left, right, dims, preferred_element_type=f32)


def split3(x):
    high = x.astype(bf16)
    rest = x - high.astype(f32)
    middle = rest.astype(bf16)
    low = (rest - middle.astype(f32)).astype(bf16)
    return high.astype(f32), middle.astype(f32), low.astype(f32)


def column_sum(x):
    return jnp.sum(x, axis=0, keepdims=True)


def row_mean(x):
    return jnp.mean(x, axis=-1, keepdims=True)


def norm_parts(x):
    centered = x - row_mean(x)
    inverse = lax.rsqrt(row_mean(centered * centered) + 1e-05)
    return centered * inverse, inverse


def norm_pull(grad, unit, inverse, gain):
    scaled = grad * gain
    return inverse * (scaled - row_mean(scaled) - unit * row_mean(scaled * unit))


def onehot8(row):
    return (lax.broadcasted_iota(jnp.int32, (8, row.shape[1]), 0) == row.astype(jnp.int32)).astype(f32)


def id_matrix(rows, row):
    return (lax.broadcasted_iota(jnp.int32, (rows, row.shape[1]), 0) == row.astype(jnp.int32)).astype(f32).astype(bf16)


def params(**kw):
    return pltpu.CompilerParams(vmem_limit_bytes=60 * MIB, **kw)


def whole(shape):
    return pl.BlockSpec(shape, lambda *_: (0,) * len(shape))


def sync(peers):
    barrier = pltpu.get_barrier_semaphore()
    for peer in peers:
        pl.semaphore_signal(barrier, inc=1, device_id=peer, device_id_type=MESH)
    pl.semaphore_wait(barrier, len(peers))


def remote(src, dst, send, recv, peer):
    return pltpu.make_async_remote_copy(
        src_ref=src, dst_ref=dst, send_sem=send, recv_sem=recv, device_id=peer, device_id_type=MESH
    )


def gather_kernel(dp_n, blk_n, mine_ref, table_ref, tok_ref, tab_ref, send, recv):
    dp = lax.axis_index("dp")
    z = lax.axis_index("blk")
    dp_peers = [(lax.rem(dp + k, dp_n), z) for k in range(1, dp_n)]
    z_peers = [(dp, lax.rem(z + k, blk_n)) for k in range(1, blk_n)]
    sync(z_peers + dp_peers)
    copies = []
    for k, peer in enumerate(z_peers):
        copies.append(remote(mine_ref, tok_ref.at[z], send.at[k], recv.at[k], peer))
    for k, peer in enumerate(dp_peers):
        n = len(z_peers) + k
        copies.append(remote(table_ref, tab_ref.at[dp], send.at[n], recv.at[n], peer))
    for c in copies:
        c.start()
    tok_ref[z] = mine_ref[...]
    tab_ref[dp] = table_ref[...]
    for c in copies:
        c.wait()


def gather(mine, table, dp_n, blk_n):
    count = dp_n + blk_n - 2
    vmem = pl.BlockSpec(memory_space=VMEM)
    return pl.pallas_call(
        functools.partial(gather_kernel, dp_n, blk_n),
        in_specs=[vmem, vmem],
        out_specs=[vmem, vmem],
        out_shape=[
            jax.ShapeDtypeStruct((blk_n,) + mine.shape, f32),
            jax.ShapeDtypeStruct((dp_n,) + table.shape, f32),
        ],
        scratch_shapes=[pltpu.SemaphoreType.DMA((count,)), pltpu.SemaphoreType.DMA((count,))],
        compiler_params=params(collective_id=0, has_side_effects=True),
        name="gather",
    )(mine, table)


class Scatter:
    def __init__(self, grad, columns, by_x, acc, first, second, third, send, recv, local):
        self.grad, self.columns, self.by_x = grad, columns, by_x
        self.acc, self.first, self.second, self.third = acc, first, second, third
        self.send, self.recv, self.local = send, recv, local
        self.dp = lax.axis_index("dp")
        self.z = lax.axis_index("blk")
        self.core = lax.rem(self.dp, 2)
        self.x = lax.rem(lax.div(self.dp, 2), 2)
        self.y = lax.div(self.dp, 4)

    def flip(self, bit, step):
        return (self.dp + step * (1 - 2 * bit), self.z)

    def core_copies(self):
        src = self.grad.at[:, :, 1 - self.core, :, self.columns]
        own = self.grad.at[:, :, self.core, :, self.columns]
        return (
            remote(src, self.first, self.send.at[0], self.recv.at[0], self.flip(self.core, 1)),
            pltpu.make_async_copy(own, self.acc, self.local),
        )

    def wide(self):
        if self.by_x:
            src, peer = self.acc.at[:, 1 - self.x], self.flip(self.x, 2)
        else:
            src, peer = self.acc.at[1 - self.y], self.flip(self.y, 4)
        return remote(src, self.second, self.send.at[1], self.recv.at[1], peer)

    def narrow(self):
        if self.by_x:
            src, peer = self.acc.at[1 - self.y, self.x], self.flip(self.y, 4)
        else:
            src, peer = self.acc.at[self.y, 1 - self.x], self.flip(self.x, 2)
        return remote(src, self.third, self.send.at[2], self.recv.at[2], peer)

    def start(self):
        for c in self.core_copies():
            c.start()

    def core_to_wide(self):
        for c in self.core_copies():
            c.wait()
        for y in range(2):
            for x in range(2):
                self.acc[y, x] = (self.acc[y, x].astype(f32) + self.first[y, x].astype(f32)).astype(bf16)
        self.wide().start()

    def wide_to_narrow(self):
        self.wide().wait()
        for n in range(2):
            at = (n, self.x) if self.by_x else (self.y, n)
            self.acc[at] = (self.acc[at].astype(f32) + self.second[n].astype(f32)).astype(bf16)
        self.narrow().start()

    def narrow_sum(self):
        self.narrow().wait()
        return self.acc[self.y, self.x].astype(f32) + self.third[...].astype(f32)


def scatter_scratch(rows, columns):
    return [
        VMEM((2, 2, rows, columns), bf16),
        VMEM((2, 2, rows, columns), bf16),
        VMEM((2, rows, columns), bf16),
        VMEM((rows, columns), bf16),
        pltpu.SemaphoreType.DMA((3,)),
        pltpu.SemaphoreType.DMA((3,)),
        pltpu.SemaphoreType.DMA,
    ]


class LineScatter:
    def __init__(self, base, out, half, first, rest, second, send, recv):
        self.base, self.out = base, out
        self.half, self.first, self.rest, self.second = half, first, rest, second
        self.send, self.recv = send, recv
        self.low = lax.rem(base.z, 2)
        self.high = lax.div(base.z, 2)

    def near(self):
        peer = (self.base.dp, self.base.z + 1 - 2 * self.low)
        return remote(self.half.at[1 - self.low], self.first, self.send.at[0], self.recv.at[0], peer)

    def far(self):
        peer = (self.base.dp, self.base.z + 2 - 4 * self.high)
        return remote(self.rest.at[1 - self.high], self.second, self.send.at[1], self.recv.at[1], peer)

    def start(self):
        total = self.base.narrow_sum()
        q = total.shape[0] // 4
        for low in range(2):
            self.half[low, :q] = total[low * q : (low + 1) * q].astype(bf16)
            self.half[low, q:] = total[(2 + low) * q : (3 + low) * q].astype(bf16)
        self.near().start()

    def near_to_far(self):
        self.near().wait()
        q = self.rest.shape[1]
        total = self.half[self.low].astype(f32) + self.first[...].astype(f32)
        self.rest[0] = total[:q]
        self.rest[1] = total[q:]
        self.far().start()

    def finish(self):
        self.far().wait()
        self.out[:, self.base.columns] = self.rest[self.high] + self.second[...]


def line_scratch(rows, columns):
    return [
        VMEM((2, rows // 2, columns), bf16),
        VMEM((rows // 2, columns), bf16),
        VMEM((2, rows // 4, columns), f32),
        VMEM((rows // 4, columns), f32),
        pltpu.SemaphoreType.DMA((2,)),
        pltpu.SemaphoreType.DMA((2,)),
    ]


UNITS = (
    (0, 0, 384, True),
    (0, 384, 384, False),
    (1, 0, 768, True),
    (1, 768, 768, False),
    (1, 1536, 768, True),
    (1, 2304, 768, False),
    (2, 0, 384, True),
    (2, 384, 384, False),
)
UNIT_ROWS = (384, 96, 96)


def embed_kernel(
    local_rows,
    z_ref,
    tok_ref,
    tab_ref,
    up_w_ref,
    vec_ref,
    w_ref,
    own_w_ref,
    own_b_ref,
    k_ref,
    vt_ref,
    own_ref,
    normed_ref,
    lhs_ref,
    sc_ref,
    qt_ref,
    h0_ref,
    rhs_ref,
    mean_ref,
    tab3,
    vcol,
):
    i = pl.program_id(0)
    dp_n, _, vp = tab_ref.shape
    blocks, _, rows = tok_ref.shape

    @pl.when(i == 0)
    def _():
        table = jnp.concatenate([tab_ref[j] for j in range(dp_n)], axis=1)
        squares = jnp.sum(table * table, axis=0, keepdims=True)
        lane = lax.broadcasted_iota(jnp.int32, squares.shape, 1)
        norms = jnp.where(lane % vp < local_rows, jnp.sqrt(squares + 1.0), 0.0)
        mean_ref[...] = jnp.broadcast_to(jnp.sum(norms, axis=1, keepdims=True) / (local_rows * dp_n), (8, 128))
        tab3[...] = jnp.concatenate(split3(table), axis=0).astype(bf16)
        segments = tok_ref[:, 17, :]
        steps = tok_ref[:, 18, :]
        sub = lax.broadcasted_iota(jnp.int32, (8, 1), 0)
        time = jnp.zeros((8, 1), f32)
        for s in range(DOCS):
            own = jnp.max(jnp.where(segments == float(s), steps, 0.0), axis=(0, 1), keepdims=True)
            time = jnp.where(sub == s, own, time)
        lane = lax.broadcasted_iota(jnp.int32, (8, D), 1)
        half = D // 2
        index = jnp.where(lane < half, lane, lane - half).astype(f32)
        angle = time * jnp.exp(index * (-math.log(10000.0) / half))
        wave = jnp.where(lane < half, jnp.sin(angle), jnp.cos(angle)) + vec_ref[0:1, :]
        parts = split3(wave)
        rhs_ref[...] = jnp.concatenate([up_w_ref[...].astype(f32), *parts, jnp.zeros((8, D), f32)], axis=0).astype(bf16)
        bias = jnp.concatenate([vec_ref[3:5, :], jnp.zeros((6, D), f32)], axis=0)
        vcol[...] = jnp.transpose(bias)

    tok = tok_ref[i]
    ids = tok[16:17, :]
    picked3 = dot(tab3[...], id_matrix(dp_n * vp, ids))
    picked = picked3[:16] + picked3[16:32] + picked3[32:48]
    mean = mean_ref[0:1, 0:1]
    alpha_bar = 1.0 - jnp.sqrt(tok[18:19, :] / TSTEPS + 0.0001)
    signal = jnp.sqrt(alpha_bar)
    noise_scale = jnp.sqrt(1.0 - alpha_bar)
    mixed = signal * (picked / mean) + noise_scale * tok[:16]
    seg = onehot8(tok[17:18, :])
    lhs = jnp.concatenate([mixed, seg, seg, seg, jnp.zeros((8, rows), f32)], axis=0).astype(bf16)
    lhs_ref[0] = lhs
    sc_ref[0] = jnp.concatenate([picked, signal, noise_scale, jnp.zeros((6, rows), f32)], axis=0)
    hidden0 = dot(lhs, rhs_ref[...], TN)
    unit, _ = norm_parts(hidden0)
    normed = (unit * vec_ref[1:2, :] + vec_ref[2:3, :]).astype(bf16)
    normed_ref[...] = normed
    k_ref[...] = dot(normed, w_ref[:, D : 2 * D]).astype(bf16)
    vt_ref[...] = (dot(w_ref[:, 2 * D :], normed, TT) + vcol[:, 1:2]).astype(bf16)
    own = dot(normed, own_w_ref[...]) + own_b_ref[...]
    own_ref[:, :SLOT] = (own[:, :SLOT] * SCALE).astype(bf16)
    own_ref[:, SLOT:] = own[:, SLOT:].astype(bf16)

    @pl.when(i == z_ref[0])
    def _():
        h0_ref[...] = hidden0
        q = (dot(w_ref[:, :D], normed, TT) + vcol[:, 0:1]).astype(bf16)
        qt_ref[...] = (q.astype(f32) * SCALE).astype(bf16)


def embed(z, tok, tab, up_w, vec, w, own_w, own_b, local_rows):
    blocks, _, rows = tok.shape
    group = blocks * rows
    vocab = tab.shape[0] * tab.shape[2]
    spec = pltpu.PrefetchScalarGridSpec(
        num_scalar_prefetch=1,
        grid=(blocks,),
        in_specs=[whole(x.shape) for x in (tok, tab, up_w, vec, w, own_w, own_b)],
        out_specs=[
            pl.BlockSpec((rows, D), lambda i, z: (i, 0)),
            pl.BlockSpec((D, rows), lambda i, z: (0, i)),
            pl.BlockSpec((rows, 3 * SLOT), lambda i, z: (i, 0)),
            pl.BlockSpec((rows, D), lambda i, z: (i, 0)),
            pl.BlockSpec((1, 48, rows), lambda i, z: (i, 0, 0)),
            pl.BlockSpec((1, 24, rows), lambda i, z: (i, 0, 0)),
            whole((D, rows)),
            whole((rows, D)),
            whole((48, D)),
            whole((8, 128)),
        ],
        scratch_shapes=[VMEM((48, vocab), bf16), VMEM((D, 8), f32)],
    )
    return pl.pallas_call(
        functools.partial(embed_kernel, local_rows),
        grid_spec=spec,
        out_shape=[
            jax.ShapeDtypeStruct((group, D), bf16),
            jax.ShapeDtypeStruct((D, group), bf16),
            jax.ShapeDtypeStruct((group, 3 * SLOT), bf16),
            jax.ShapeDtypeStruct((group, D), bf16),
            jax.ShapeDtypeStruct((blocks, 48, rows), bf16),
            jax.ShapeDtypeStruct((blocks, 24, rows), f32),
            jax.ShapeDtypeStruct((D, rows), bf16),
            jax.ShapeDtypeStruct((rows, D), f32),
            jax.ShapeDtypeStruct((48, D), bf16),
            jax.ShapeDtypeStruct((8, 128), f32),
        ],
        compiler_params=params(),
        name="embed",
    )(z, tok, tab, up_w, vec, w, own_w, own_b)


ROOT = math.sqrt(2.0 / math.pi)


def layer_kernel(
    per,
    tok_ref,
    mine_ref,
    k_ref,
    vt_ref,
    qt_ref,
    h0_ref,
    cot_ref,
    vec_ref,
    b1_ref,
    wo_ref,
    w1_ref,
    w2_ref,
    out_ref,
    h1g_ref,
    msg_ref,
    dwo_ref,
    dw1_ref,
    dw2_ref,
    small_ref,
    kext,
    qext,
    att,
    lse,
    wo,
    wo_slots,
    w1,
    w2,
    sems,
):
    p = pl.program_id(0)
    last = pl.num_programs(0) - 1
    blocks, _, rows = tok_ref.shape
    copies = [
        pltpu.make_async_copy(wo_ref, wo, sems.at[0]),
        pltpu.make_async_copy(w1_ref, w1, sems.at[1]),
        pltpu.make_async_copy(w2_ref, w2, sems.at[2]),
    ]

    @pl.when(p == 0)
    def _():
        for c in copies:
            c.start()
        for b in range(blocks):
            seg = jnp.concatenate([onehot8(tok_ref[b, 17:18, :]), jnp.zeros((120, rows), f32)], axis=0)
            kext[b * rows : (b + 1) * rows, :] = jnp.transpose(seg).astype(bf16)
        seg = onehot8(mine_ref[17:18, :])
        sub = lax.broadcasted_iota(jnp.int32, seg.shape, 0)
        barred = jnp.where(sub < DOCS, -BIG * (1.0 - seg), 0.0)
        qext[...] = jnp.concatenate([barred, jnp.zeros((120, rows), f32)], axis=0).astype(bf16)

    keys = jnp.concatenate([k_ref[...], kext[...]], axis=1)
    zeros = jnp.zeros((HEAD_DIM, rows), bf16)
    ones = jnp.ones((HEAD_DIM, blocks * rows), bf16)
    results = []
    for h in range(2):
        q = qt_ref[h * HEAD_DIM : (h + 1) * HEAD_DIM, :]
        v = vt_ref[h * HEAD_DIM : (h + 1) * HEAD_DIM, :]
        queries = jnp.concatenate([q, zeros, qext[...]] if h == 0 else [zeros, q, qext[...]], axis=0)
        scores = dot(keys, queries)
        top = jnp.max(scores, axis=0, keepdims=True)
        weights = jnp.exp(scores - top).astype(bf16)
        total = dot(jnp.concatenate([v, ones], axis=0), weights)
        results.append(total[:HEAD_DIM] / total[HEAD_DIM:])
        lse[pl.ds(2 * p + h, 1), :] = top + jnp.log(total[HEAD_DIM : HEAD_DIM + 1])
    att[pl.ds(pl.multiple_of(p * PAIR, PAIR), PAIR), :] = jnp.concatenate(results, axis=0)

    @pl.when(p == last)
    def _():
        for c in copies:
            c.wait()
        attended = att[...].astype(bf16)
        hidden1 = h0_ref[...] + dot(attended, wo[...], TN) + vec_ref[0:1, :]
        unit, inverse = norm_parts(hidden1)
        normed2 = (unit * vec_ref[1:2, :] + vec_ref[2:3, :]).astype(bf16)
        cot = cot_ref[...]
        out_grad = cot.astype(bf16)
        block_out = hidden1 + vec_ref[3:4, :]
        norm_grad = jnp.zeros_like(hidden1)
        inner_sums = []
        for c in range(FF // D):
            cols = slice(c * D, (c + 1) * D)
            x = dot(normed2, w1[:, cols]) + b1_ref[c : c + 1, :]
            square = x * x
            t = jnp.tanh(x * (ROOT + (ROOT * 0.044715) * square))
            half = 0.5 * (1.0 + t)
            active = (x * half).astype(bf16)
            slope = half + (0.5 * x) * (1.0 - t * t) * (ROOT + (3.0 * ROOT * 0.044715) * square)
            block_out = block_out + dot(active, w2[cols, :])
            inner_grad = (dot(out_grad, w2[cols, :], NT) * slope).astype(bf16)
            dw2_ref[cols, :] = dot(active, out_grad, TN).astype(bf16)
            dw1_ref[:, cols] = dot(normed2, inner_grad, TN).astype(bf16)
            norm_grad = norm_grad + dot(inner_grad, w1[:, cols], NT)
            inner_sums.append(column_sum(inner_grad.astype(f32)))
        out_ref[...] = block_out
        hidden1_grad = cot + norm_pull(norm_grad, unit, inverse, vec_ref[1:2, :])
        h1g_ref[...] = hidden1_grad
        branch = hidden1_grad.astype(bf16)
        dwo_ref[...] = dot(attended, branch).astype(bf16)
        small_ref[...] = jnp.concatenate(
            [
                column_sum(branch.astype(f32)),
                column_sum(norm_grad * unit),
                column_sum(norm_grad),
                column_sum(out_grad.astype(f32)),
                *inner_sums,
            ],
            axis=0,
        )
        seg = onehot8(mine_ref[17:18, :])
        back = dot(wo[...], branch, NT).astype(bf16).astype(f32)
        product = back * att[...]
        for j in range(blocks):
            heads = [h for h in range(per * j, per * (j + 1)) if h < HEADS]
            wo_slots[...] = jnp.zeros_like(wo_slots)
            size = len(heads) * HEAD_DIM
            rows_ext = [jnp.zeros((HEAD_DIM, rows), f32), jnp.where(
                lax.broadcasted_iota(jnp.int32, (8, rows), 0) < DOCS, -BIG * (1.0 - seg), 0.0
            )[:DOCS]]
            lse_parts = []
            delta_parts = []
            for n in range(3):
                h = per * j + n
                if n < per and h < HEADS:
                    delta = column_sum(product[h * HEAD_DIM : (h + 1) * HEAD_DIM])
                    lse_parts += split3(-lse[h : h + 1, :])
                    delta_parts += split3(-delta)
                else:
                    lse_parts += [jnp.zeros((1, rows), f32)] * 3
                    delta_parts += [jnp.zeros((1, rows), f32)] * 3
            used = DOCS + 18
            rows_ext = rows_ext + lse_parts + delta_parts + [jnp.zeros((HEAD_DIM - used, rows), f32)]
            ext = jnp.transpose(jnp.concatenate(rows_ext, axis=0))
            if size:
                wo_slots[:size, :] = wo[heads[0] * HEAD_DIM : heads[0] * HEAD_DIM + size, :]
            grads = dot(branch, wo_slots[...], NT)
            msg_ref[j, :, :PAIR] = grads[:, :PAIR].astype(bf16)
            msg_ref[j, :, PAIR:] = (grads[:, PAIR:] + ext).astype(bf16)


def layer(tok, mine, k, vt, qt, h0, cot, vec, b1, wo, w1, w2, per):
    blocks, _, rows = tok.shape
    group = blocks * rows
    any_spec = pl.BlockSpec(memory_space=pl.ANY)
    return pl.pallas_call(
        functools.partial(layer_kernel, per),
        grid=(HEADS // 2,),
        in_specs=[
            whole(tok.shape),
            whole(mine.shape),
            pl.BlockSpec((group, PAIR), lambda p: (0, p)),
            pl.BlockSpec((PAIR, group), lambda p: (p, 0)),
            pl.BlockSpec((PAIR, rows), lambda p: (p, 0)),
            whole(h0.shape),
            whole(cot.shape),
            whole(vec.shape),
            whole(b1.shape),
            any_spec,
            any_spec,
            any_spec,
        ],
        out_specs=[
            whole((rows, D)),
            whole((rows, D)),
            whole((blocks, rows, SLOT)),
            whole((D, D)),
            whole((D, FF)),
            whole((FF, D)),
            whole((8, D)),
        ],
        out_shape=[
            jax.ShapeDtypeStruct((rows, D), f32),
            jax.ShapeDtypeStruct((rows, D), f32),
            jax.ShapeDtypeStruct((blocks, rows, SLOT), bf16),
            jax.ShapeDtypeStruct((D, D), bf16),
            jax.ShapeDtypeStruct((D, FF), bf16),
            jax.ShapeDtypeStruct((FF, D), bf16),
            jax.ShapeDtypeStruct((8, D), f32),
        ],
        scratch_shapes=[
            VMEM((group, PAIR), bf16),
            VMEM((PAIR, rows), bf16),
            VMEM((D, rows), f32),
            VMEM((16, rows), f32),
            VMEM((D, D), bf16),
            VMEM((SLOT, D), bf16),
            VMEM((D, FF), bf16),
            VMEM((FF, D), bf16),
            pltpu.SemaphoreType.DMA((3,)),
        ],
        compiler_params=params(),
        name="layer",
    )(tok, mine, k, vt, qt, h0, cot, vec, b1, wo, w1, w2)


def back_prepare(per, tok_ref, own_ref, kt, vt, ksel):
    blocks, _, rows = tok_ref.shape
    for b in range(blocks):
        place = slice(b * rows, (b + 1) * rows)
        seg = onehot8(tok_ref[b, 17:18, :])
        sub = lax.broadcasted_iota(jnp.int32, (HEAD_DIM, rows), 0)
        seg64 = jnp.concatenate([seg, jnp.zeros((HEAD_DIM - 8, rows), f32)], axis=0)
        kb = own_ref[place, SLOT : 2 * SLOT]
        kt_b = jnp.transpose(kb.astype(f32))
        vt_b = jnp.transpose(own_ref[place, 2 * SLOT :].astype(f32))
        lane = lax.broadcasted_iota(jnp.int32, kb.shape, 1)
        row = lax.broadcasted_iota(jnp.int32, kt_b.shape, 0)
        for h in range(per):
            inside = (row >= h * HEAD_DIM) & (row < (h + 1) * HEAD_DIM)
            first = DOCS + 3 * h
            k_ext = jnp.where((sub >= first) & (sub < first + 3), 1.0, jnp.where(sub < DOCS, seg64, 0.0))
            first = DOCS + 9 + 3 * h
            v_ext = jnp.where((sub >= first) & (sub < first + 3), 1.0, 0.0)
            kt[h, :, place] = jnp.concatenate([jnp.where(inside, kt_b, 0.0)[:EXT], k_ext], axis=0).astype(bf16)
            vt[h, :, place] = jnp.concatenate([jnp.where(inside, vt_b, 0.0)[:EXT], v_ext], axis=0).astype(bf16)
            mine = (lane >= h * HEAD_DIM) & (lane < (h + 1) * HEAD_DIM)
            ksel[h, place, :] = jnp.where(mine, kb.astype(f32), 0.0).astype(bf16)


def back_block(per, q, msg, kt, vt, ksel, dkt, dvt):
    lane = lax.broadcasted_iota(jnp.int32, q.shape, 1)
    queries = jnp.where(lane < EXT, q.astype(f32), msg.astype(f32)).astype(bf16)
    q_t = jnp.transpose(q.astype(f32)).astype(bf16)
    m_t = jnp.transpose(msg.astype(f32)).astype(bf16)
    dq = jnp.zeros(q.shape, f32)
    for h in range(per):
        head = slice(h * HEAD_DIM, (h + 1) * HEAD_DIM)
        probs = jnp.exp(dot(queries, kt[h]))
        score_grad = (probs * dot(msg, vt[h])).astype(bf16)
        dvt[head, :] += dot(m_t[head], probs.astype(bf16))
        dkt[head, :] += dot(q_t[head], score_grad)
        dq = dq + dot(score_grad, ksel[h])
    return (dq * SCALE).astype(bf16)


def back_kernel(per, tok_ref, own_ref, msg_ref, grad_ref, kt, vt, ksel, dkt, dvt):
    blocks, _, rows = tok_ref.shape
    back_prepare(per, tok_ref, own_ref, kt, vt, ksel)
    dkt[...] = jnp.zeros_like(dkt)
    dvt[...] = jnp.zeros_like(dvt)

    def step(b, carry):
        place = pl.ds(pl.multiple_of(b * rows, rows), rows)
        grad_ref[place, :SLOT] = back_block(per, own_ref[place, :SLOT], msg_ref[b], kt, vt, ksel, dkt, dvt)
        return carry

    lax.fori_loop(0, blocks, step, 0)
    for b in range(blocks):
        place = slice(b * rows, (b + 1) * rows)
        grad_ref[place, SLOT : 2 * SLOT] = jnp.transpose(dkt[:, place]).astype(bf16)
        grad_ref[place, 2 * SLOT :] = jnp.transpose(dvt[:, place]).astype(bf16)


def back(tok, own, msg, per):
    group = own.shape[0]
    return pl.pallas_call(
        functools.partial(back_kernel, per),
        in_specs=[pl.BlockSpec(memory_space=VMEM)] * 3,
        out_specs=pl.BlockSpec(memory_space=VMEM),
        out_shape=jax.ShapeDtypeStruct(own.shape, bf16),
        scratch_shapes=[
            VMEM((per, SLOT, group), bf16),
            VMEM((per, SLOT, group), bf16),
            VMEM((per, group, SLOT), bf16),
            VMEM((SLOT, group), f32),
            VMEM((SLOT, group), f32),
        ],
        compiler_params=params(),
        name="attention_back",
    )(tok, own, msg)


def back_scatter_kernel(
    per, plan, tok_ref, own_ref, msg_ref, dw2_ref, dw1_ref, dwo_ref, grad_ref, dw2_out, dw1_out, dwo_out,
    kt, vt, ksel, dkt, dvt, msgs, msg_send, msg_recv, *scratch
):
    blocks, _, rows = tok_ref.shape
    dp = lax.axis_index("dp")
    z = lax.axis_index("blk")
    grads = (dw2_ref, dw1_ref, dwo_ref)
    outs = (dw2_out, dw1_out, dwo_out)
    units = []
    for n, (which, first, size, by_x) in enumerate(UNITS):
        part = scratch[13 * n : 13 * (n + 1)]
        base = Scatter(grads[which], pl.ds(first, size), by_x, *part[:7])
        units.append((base, LineScatter(base, outs[which], *part[7:])))
    core, x, y = units[0][0].core, units[0][0].x, units[0][0].y

    def z_peer(k):
        low, high = lax.rem(z, 2), lax.div(z, 2)
        return (low + (k % 2) * (1 - 2 * low)) + 2 * (high + (k // 2) * (1 - 2 * high))

    base = units[0][0]
    sync([base.flip(core, 1), base.flip(x, 2), base.flip(y, 4)] + [(dp, z_peer(k)) for k in range(1, blocks)])

    def message(k):
        return remote(msg_ref.at[z_peer(k)], msgs.at[k], msg_send.at[k], msg_recv.at[k], (dp, z_peer(k)))

    for k in (1, 2, 3):
        message(k).start()

    def run(step):
        kind, n = step
        base, line = units[n]
        if kind == 0:
            base.start()
        elif kind == 1:
            base.core_to_wide()
        elif kind == 2:
            base.wide_to_narrow()
        elif kind == 3:
            line.start()
        elif kind == 4:
            line.near_to_far()
        else:
            line.finish()

    for step in plan[0]:
        run(step)
    back_prepare(per, tok_ref, own_ref, kt, vt, ksel)
    dkt[...] = jnp.zeros_like(dkt)
    dvt[...] = jnp.zeros_like(dvt)
    msgs[0] = msg_ref[z]
    for step in plan[1]:
        run(step)

    def body(b, carry):
        low, high = lax.rem(z, 2), lax.div(z, 2)
        b_low, b_high = lax.rem(b, 2), lax.div(b, 2)
        other = (low + b_low * (1 - 2 * low)) + 2 * (high + b_high * (1 - 2 * high))
        for k in range(1, blocks):

            @pl.when(b == k)
            def _():
                message(k).wait()

        for k in range(blocks):
            if plan[2 + k]:

                @pl.when(b == k)
                def _():
                    for step in plan[2 + k]:
                        run(step)

        place = pl.ds(pl.multiple_of(other * rows, rows), rows)
        grad_ref[place, :SLOT] = back_block(per, own_ref[place, :SLOT], msgs[b], kt, vt, ksel, dkt, dvt)
        return carry

    lax.fori_loop(0, blocks, body, 0)
    for step in plan[6]:
        run(step)
    for b in range(blocks):
        place = slice(b * rows, (b + 1) * rows)
        grad_ref[place, SLOT : 2 * SLOT] = jnp.transpose(dkt[:, place]).astype(bf16)
        grad_ref[place, 2 * SLOT :] = jnp.transpose(dvt[:, place]).astype(bf16)
    for step in plan[7]:
        run(step)


ALL = range(8)
PLAN = (
    [(0, n) for n in ALL],
    [(1, n) for n in (0, 1)],
    [(1, n) for n in range(2, 8)],
    [],
    [(2, 0), (2, 1)],
    [(2, 2), (2, 3), (3, 0), (3, 1)],
    [(2, 4), (2, 5), (4, 0), (4, 1), (3, 2), (3, 3), (2, 6), (2, 7)],
    [(3, 4), (3, 5), (5, 0), (5, 1), (4, 2), (4, 3), (3, 6), (3, 7), (4, 4), (4, 5), (4, 6), (4, 7)]
    + [(5, n) for n in range(2, 8)],
)


def back_scatter(tok, own, msg, dw2, dw1, dwo, per):
    blocks, rows = msg.shape[:2]
    group = own.shape[0]
    vmem = pl.BlockSpec(memory_space=VMEM)
    hbm = pl.BlockSpec(memory_space=pl.ANY)
    scratch = []
    for which, _, size, _ in UNITS:
        scratch += scatter_scratch(UNIT_ROWS[which], size) + line_scratch(UNIT_ROWS[which], size)
    return pl.pallas_call(
        functools.partial(back_scatter_kernel, per, PLAN),
        in_specs=[vmem] * 3 + [hbm] * 3,
        out_specs=[vmem] * 4,
        out_shape=[
            jax.ShapeDtypeStruct(own.shape, bf16),
            jax.ShapeDtypeStruct((96, D), f32),
            jax.ShapeDtypeStruct((24, FF), f32),
            jax.ShapeDtypeStruct((24, D), f32),
        ],
        scratch_shapes=[
            VMEM((per, SLOT, group), bf16),
            VMEM((per, SLOT, group), bf16),
            VMEM((per, group, SLOT), bf16),
            VMEM((SLOT, group), f32),
            VMEM((SLOT, group), f32),
            VMEM((blocks, rows, SLOT), bf16),
            pltpu.SemaphoreType.DMA((blocks,)),
            pltpu.SemaphoreType.DMA((blocks,)),
            *scratch,
        ],
        compiler_params=params(collective_id=1, has_side_effects=True),
        name="attention_back_scatter",
    )(
        tok,
        own,
        msg,
        dw2.reshape(2, 2, 2, 384, D),
        dw1.reshape(2, 2, 2, 96, FF),
        dwo.reshape(2, 2, 2, 96, D),
    )


def final_kernel(
    z_ref, tok_ref, grad_ref, normed_ref, lhs_ref, sc_ref, rhs_ref, h1g_ref, up_w_ref, vec_ref, own_w_ref, mean_ref,
    dw_ref, noise_ref, table_ref, small_ref, acc,
):
    i = pl.program_id(0)
    last = pl.num_programs(0) - 1
    vocab = table_ref.shape[1]
    mean = mean_ref[0:1, 0:1]

    @pl.when(i == 0)
    def _():
        acc[...] = jnp.zeros_like(acc)
        small_ref[...] = jnp.zeros_like(small_ref)
        table_ref[...] = jnp.zeros_like(table_ref)

    grad = grad_ref[...]
    hidden0 = dot(lhs_ref[0], rhs_ref[...], TN)
    unit, inverse = norm_parts(hidden0)
    norm_grad = dot(grad, own_w_ref[...], NT)
    acc[...] += dot(normed_ref[...], grad, TN)
    own = (z_ref[0] == i).astype(f32)
    h0_grad = (norm_pull(norm_grad, unit, inverse, vec_ref[1:2, :]) + own * h1g_ref[...]).astype(bf16)
    mixed_grad = dot(up_w_ref[...], h0_grad, NT)
    sc = sc_ref[0]
    noise_ref[0] = sc[17:18] * mixed_grad
    embedded_grad = sc[16:17] * mixed_grad
    picked = sc[:16]
    norm_term = -jnp.sum(embedded_grad * picked, axis=(0, 1), keepdims=True) / (mean * mean)
    ids = tok_ref[i][16:17, :]
    table3 = dot(jnp.concatenate(split3(embedded_grad / mean), axis=0).astype(bf16), id_matrix(vocab, ids), NT)
    table_ref[...] += table3[:16] + table3[16:32] + table3[32:48]
    gradf = grad.astype(f32)
    small_ref[...] += jnp.concatenate(
        [
            dot(lhs_ref[0, :16, :], h0_grad),
            column_sum(h0_grad.astype(f32)),
            column_sum(norm_grad * unit),
            column_sum(norm_grad),
            column_sum(gradf),
            jnp.broadcast_to(norm_term, (1, D)),
            jnp.zeros((3, D), f32),
        ],
        axis=0,
    )

    @pl.when(i == last)
    def _():
        dw_ref[...] = acc[...].astype(bf16)


def final(z, tok, grad, normed, lhs, sc, rhs, h1g, up_w, vec, own_w, mean, vocab):
    blocks, _, rows = tok.shape
    spec = pltpu.PrefetchScalarGridSpec(
        num_scalar_prefetch=1,
        grid=(blocks,),
        in_specs=[
            whole(tok.shape),
            pl.BlockSpec((rows, 3 * SLOT), lambda i, z: (i, 0)),
            pl.BlockSpec((rows, D), lambda i, z: (i, 0)),
            pl.BlockSpec((1, 48, rows), lambda i, z: (i, 0, 0)),
            pl.BlockSpec((1, 24, rows), lambda i, z: (i, 0, 0)),
            whole(rhs.shape),
            whole(h1g.shape),
            whole(up_w.shape),
            whole(vec.shape),
            whole(own_w.shape),
            whole(mean.shape),
        ],
        out_specs=[
            whole((D, 3 * SLOT)),
            pl.BlockSpec((1, 16, rows), lambda i, z: (i, 0, 0)),
            whole((16, vocab)),
            whole((24, D)),
        ],
        scratch_shapes=[VMEM((D, 3 * SLOT), f32)],
    )
    return pl.pallas_call(
        final_kernel,
        grid_spec=spec,
        out_shape=[
            jax.ShapeDtypeStruct((D, 3 * SLOT), bf16),
            jax.ShapeDtypeStruct((blocks, 16, rows), f32),
            jax.ShapeDtypeStruct((16, vocab), f32),
            jax.ShapeDtypeStruct((24, D), f32),
        ],
        compiler_params=params(),
        name="embed_back",
    )(z, tok, grad, normed, lhs, sc, rhs, h1g, up_w, vec, own_w, mean)


def tail_kernel(
    dw_ref, small_ref, noise_ref, dw_out, small_out, table_out, noise_out,
    parts, mine, lines, sums, dw_parts, dw_mine, noise_parts, sends, recvs, *scratch
):
    dp = lax.axis_index("dp")
    z = lax.axis_index("blk")
    dp_n, blk_n = parts.shape[0], lines.shape[0]
    half = D // 2
    units = [
        Scatter(dw_ref, pl.ds(0, half), True, *scratch[:7]),
        Scatter(dw_ref, pl.ds(half, half), False, *scratch[7:]),
    ]
    dp_to = [(lax.rem(dp + k, dp_n), z) for k in range(1, dp_n)]
    z_to = [(dp, lax.rem(z + k, blk_n)) for k in range(1, blk_n)]
    sync(dp_to + z_to)
    nd, nz = dp_n - 1, blk_n - 1

    def spread(src, dst, peers, first):
        return [
            remote(src(p), dst, sends.at[first + k], recvs.at[first + k], p) for k, p in enumerate(peers)
        ]

    for u in units:
        u.start()
    one = spread(lambda p: small_ref.at[p[0]], parts.at[dp], dp_to, 0)
    four = spread(lambda p: noise_ref.at[p[1]], noise_parts.at[z], z_to, 2 * nd + nz)
    for c in one + four:
        c.start()
    parts[dp] = small_ref[dp]
    noise_parts[z] = noise_ref[z]
    for u in units:
        u.core_to_wide()
    for c in one:
        c.wait()
    total = parts[0]
    for k in range(1, dp_n):
        total = total + parts[k]
    mine[...] = total
    lines[z] = total
    two = spread(lambda p: mine, lines.at[z], z_to, nd)
    for c in two:
        c.start()
    for u in units:
        u.wide_to_narrow()
    for c in two:
        c.wait()
    total = lines[0]
    for k in range(1, blk_n):
        total = total + lines[k]
    table_out[...] = total[:, half:]
    sums[...] = total[:, :half]
    small_out[dp] = total[:, :half]
    three = spread(lambda p: sums, small_out.at[dp], dp_to, nd + nz)
    for c in three:
        c.start()
    for u in units:
        total = u.narrow_sum()
        q = total.shape[0] // blk_n
        for k in range(blk_n):
            dw_parts[k, :, u.columns] = total[k * q : (k + 1) * q]
    five = spread(lambda p: dw_parts.at[p[1]], dw_out.at[z], z_to, 2 * nd + 2 * nz)
    for c in five:
        c.start()
    dw_out[z] = dw_parts[z]
    for c in four:
        c.wait()
    total = noise_parts[0]
    for k in range(1, blk_n):
        total = total + noise_parts[k]
    noise_out[...] = total
    for c in three + five:
        c.wait()


def tail(dw, small, noise, dp_n, blk_n):
    rows = noise.shape[2]
    share = D // (dp_n * blk_n)
    vmem = pl.BlockSpec(memory_space=VMEM)
    width = small.shape[2]
    count = 2 * (dp_n - 1) + 3 * (blk_n - 1)
    half = D // 2
    return pl.pallas_call(
        tail_kernel,
        in_specs=[vmem] * 3,
        out_specs=[vmem] * 4,
        out_shape=[
            jax.ShapeDtypeStruct((blk_n, share, 3 * SLOT), f32),
            jax.ShapeDtypeStruct((dp_n, 8, half), f32),
            jax.ShapeDtypeStruct((8, width - half), f32),
            jax.ShapeDtypeStruct((16, rows), f32),
        ],
        scratch_shapes=[
            VMEM((dp_n, 8, width), f32),
            VMEM((8, width), f32),
            VMEM((blk_n, 8, width), f32),
            VMEM((8, half), f32),
            VMEM((blk_n, share, 3 * SLOT), f32),
            VMEM((8, 128), f32),
            VMEM((blk_n, 16, rows), f32),
            pltpu.SemaphoreType.DMA((count,)),
            pltpu.SemaphoreType.DMA((count,)),
            *(scatter_scratch(D // dp_n, half) * 2),
        ],
        compiler_params=params(collective_id=2, has_side_effects=True),
        name="tail",
    )(dw.reshape(2, 2, 2, D // dp_n, 3 * SLOT), small, noise)


def shards(
    dp_n,
    blk_n,
    token_ids,
    segment_ids,
    timesteps,
    noise,
    table,
    up_weight,
    up_bias,
    norm1_gain,
    norm1_shift,
    qkv_weight,
    query_bias,
    value_bias,
    out_weight,
    out_bias,
    norm2_gain,
    norm2_shift,
    ffn_in_weight,
    ffn_in_bias,
    ffn_out_weight,
    ffn_out_bias,
    cotangent,
):
    rows = token_ids.shape[0]
    local_rows = table.shape[0]
    vp = -(-local_rows // 128) * 128
    per = -(-HEADS // blk_n)
    width = per * HEAD_DIM
    z = lax.axis_index("blk")
    z1 = z.reshape(1).astype(jnp.int32)

    slots = (token_ids // local_rows) * vp + token_ids % local_rows
    scalars = jnp.stack([slots, segment_ids, timesteps]).astype(f32)
    mine = jnp.concatenate([noise.T, scalars, jnp.zeros((5, rows), f32)], axis=0)
    tab_mine = jnp.pad(table.T, ((0, 0), (0, vp - local_rows)))
    near = dp_n == 8 and blk_n == 4
    if near:
        tok, tab = gather(mine, tab_mine, dp_n, blk_n)
    else:
        tok = lax.all_gather(mine, "blk")
        tab = lax.all_gather(tab_mine, "dp")

    padded = blk_n * width
    split = jnp.pad(qkv_weight.reshape(D, 3, D), ((0, 0), (0, 0), (0, padded - D)))
    own_w = lax.dynamic_slice(split, (0, 0, z * width), (D, 3, width))
    own_w = jnp.pad(own_w, ((0, 0), (0, 0), (0, SLOT - width))).reshape(D, 3 * SLOT)
    bias = jnp.pad(jnp.stack([query_bias, jnp.zeros((D,), f32), value_bias]), ((0, 0), (0, padded - D)))
    own_b = lax.dynamic_slice(bias, (0, z * width), (3, width))
    own_b = jnp.pad(own_b, ((0, 0), (0, SLOT - width))).reshape(1, 3 * SLOT)
    vec1 = jnp.stack([up_bias, norm1_gain, norm1_shift, query_bias, value_bias])
    k, vt, own, normed, lhs, sc, qt, h0, rhs, mean = embed(
        z1, tok, tab, up_weight, vec1, qkv_weight, own_w, own_b, local_rows
    )
    vec2 = jnp.stack([out_bias, norm2_gain, norm2_shift, ffn_out_bias])
    b1 = ffn_in_bias.reshape(FF // D, D)
    block_out, h1g, msg, dwo, dw1, dw2, small1 = layer(
        tok, mine, k, vt, qt, h0, cotangent, vec2, b1, out_weight, ffn_in_weight, ffn_out_weight, per
    )
    if near:
        grad, dw2, dw1, dwo = back_scatter(tok, own, msg, dw2, dw1, dwo, per)
    else:
        msg = lax.all_to_all(msg, "blk", 0, 0)
        grad = back(tok, own, msg, per)
    dw, noise_part, table_part, small2 = final(
        z1, tok, grad, normed, lhs, sc, rhs, h1g, up_weight, vec1, own_w, mean, dp_n * vp
    )
    share = D // (dp_n * blk_n)
    if near:
        place = (jnp.arange(blk_n) == z).astype(f32)[:, None]
        flat = jnp.concatenate([small1, small2[:19], small2[20:21], place * small2[19:20]], axis=0)
        flat = jnp.concatenate([flat[:, : D // 2], flat[:, D // 2 :]], axis=0).reshape(dp_n, 8, D // 2)
        table_part = table_part.reshape(2, 8, dp_n, vp).transpose(2, 1, 0, 3).reshape(dp_n, 8, 2 * vp)
        dw, flat, table_total, noise_grad = tail(dw, jnp.concatenate([flat, table_part], axis=2), noise_part, dp_n, blk_n)
        noise_grad = noise_grad.T
        flat = flat.reshape(-1, D // 2)
        flat = jnp.concatenate([flat[:32], flat[32:]], axis=1)
        small1, small2 = flat[:8], flat[8:28]
        norm_grad = flat[27, 0]
        own_sums = flat[28:32].reshape(blk_n, 3, SLOT)[:, :, :width].transpose(1, 0, 2).reshape(3, padded)
        table_grad = table_total.reshape(8, 2, vp).transpose(1, 0, 2).reshape(16, vp)
    else:
        noise_grad = lax.psum_scatter(noise_part, "blk", scatter_dimension=0, tiled=False).T
        own_sums = small2[19].reshape(3, SLOT)[:, :width]
        own_sums = lax.dynamic_update_slice(jnp.zeros((3, padded), f32), own_sums, (0, z * width))[:, :D]
        small2, table_total, small1, own_sums = lax.psum((small2, table_part, small1, own_sums), ("dp", "blk"))
        scatter = functools.partial(lax.psum_scatter, axis_name=("dp", "blk"), scatter_dimension=0, tiled=True)
        dwo, dw1, dw2 = scatter(dwo), scatter(dw1), scatter(dw2)
        dw = lax.psum_scatter(dw, "dp", scatter_dimension=0, tiled=True)
        dw = lax.all_to_all(dw.reshape(blk_n, share, 3 * SLOT), "blk", 0, 0)
        norm_grad = small2[20, 0]
        table_grad = lax.dynamic_slice(table_total, (0, lax.axis_index("dp") * vp), (16, vp))
    dw = dw.reshape(blk_n, share, 3, SLOT)[..., :width].transpose(1, 2, 0, 3).reshape(share, 3, padded)[..., :D]
    qkv_weight_grad = dw.reshape(share, 3 * D).astype(f32)
    mean_norm = mean[0, 0]
    table_grad = table_grad[:, :local_rows].T
    norms = jnp.sqrt(jnp.sum(table * table, axis=-1, keepdims=True) + 1.0)
    table_grad = table_grad + norm_grad * table / (dp_n * local_rows * norms)
    return (
        block_out,
        noise_grad,
        table_grad,
        small2[:16],
        small2[16],
        small2[17],
        small2[18],
        qkv_weight_grad,
        own_sums[0],
        own_sums[2],
        dwo.astype(f32),
        small1[0],
        small1[1],
        small1[2],
        dw1.astype(f32),
        small1[4:8].reshape(FF),
        dw2.astype(f32),
        small1[3],
        mean_norm,
    )


def solution(mesh):
    rows = P(("dp", "blk"))
    wide = P(("dp", "blk"), None)
    in_specs = (rows, rows, rows, wide, P("dp", None)) + (P(),) * 15 + (wide,)
    out_specs = (
        (wide, wide, P("dp", None))
        + (P(),) * 4
        + (wide, P(), P(), wide, P(), P(), P(), wide, P(), wide, P(), P())
    )
    body = functools.partial(shards, mesh.shape["dp"], mesh.shape["blk"])
    return jax.shard_map(body, mesh=mesh, in_specs=in_specs, out_specs=out_specs, check_vma=False)
```

time: 1050 us -> 251 us (0.24)
  waiting for transfers between devices: 609 us -> 0 us
  Pallas kernels: 0 us -> 217 us
  matrix products: 210 us -> 0 us
  blocking collectives: 81.9 us -> 0 us
  local copies, waits for them, and re-layouts: 77.3 us -> 21.4 us
  other arithmetic: 42.1 us -> 7.08 us
  between operations: 18.9 us -> 1.26 us
    reduce_scatter x5 -> x0, waiting for transfers between devices: 512 us -> none  [the longest x1 142 us: shards(): lax.psum_scatter(outer_weight_term, ('dp', 'blk'), scatter_dimension=0, t...]
    pallas_call x0 -> x6, Pallas kernels: none -> 217 us  [the longest x1 86.8 us: back_scatter(): pl.pallas_call(functools.partial(back_scatter_kernel, per, PLAN), in_spec...]
    dot_general x45 -> x0, matrix products: 210 us -> none  [the longest x8 45 us: visit(): jnp.einsum('rhd,khd->rhk', query_heads, key_part, preferred_element_type=...]
    all_gather x2 -> x0, waiting for transfers between devices: 96.5 us -> none  [the longest x1 48.5 us: shards(): key_rows = lax.all_gather(keys, 'blk', axis=0, tiled=True)]
    psum x2 -> x0, blocking collectives: 60.8 us -> none  [the longest x1 45.1 us: shards(): lax.psum((up_weight_term, up_bias_term, gain_one_term, shift_one_term, qu...]
    reduce_sum x14 -> x1, other arithmetic: 24.5 us -> 0.02 us  [shards(): norms = jnp.sqrt(jnp.sum(table * table, axis=-1, keepdims=True) + 1.0)]
    all_gather x2 -> x0, blocking collectives: 21.1 us -> none  [the longest x1 12.7 us: shards(): segment_all = lax.all_gather(segment_ids, 'blk', axis=0, tiled=True)]
    dynamic_update_slice x8 -> x0, local copies, waits for them, and re-layouts: 21 us -> none  [attend_backward(): lax.scan(visit, start_grad, key_blocks(key_rows, value_rows, key_segments))]
  transfers between devices with their start and end apart: 7 -> 0, of which waited for: 7 -> 0; matrix products, arithmetic and copies ran while one was open for 8% -> 0% of each run, Pallas kernels for 0% -> 0%
where the time goes in v1:
time: 251 us; the launch traced here: 247 us
  Pallas kernels  217 us (86%)
  local copies, waits for them, and re-layouts  21.4 us (9%)
  other arithmetic  7.08 us (3%)
    pallas_call x1, Pallas kernels, back_scatter(): pl.pallas_call(functools.partial(back_scatter_kernel, per, PLAN), in_spec...  86.8 us
    pallas_call x1, Pallas kernels, layer(): pl.pallas_call(functools.partial(layer_kernel, per), grid=(HEADS // 2,),...  62 us
    pallas_call x1, Pallas kernels, tail(): pl.pallas_call(tail_kernel, in_specs=[vmem] * 3, out_specs=[vmem] * 4, ou...  22.5 us
    pallas_call x1, Pallas kernels, embed(): pl.pallas_call(functools.partial(embed_kernel, local_rows), grid_spec=spe...  17.8 us
    pallas_call x1, Pallas kernels, final(): pl.pallas_call(final_kernel, grid_spec=spec, out_shape=[jax.ShapeDtypeStr...  15.2 us
    pallas_call x1, Pallas kernels, gather(): pl.pallas_call(functools.partial(gather_kernel, dp_n, blk_n), in_specs=[v...  12.8 us
    unnamed x39, local copies, waits for them, and re-layouts  7.87 us

profile of v1, /device:TPU:0, one launch (start us, length us, event | category | flops | bytes accessed | tf_op | source)
XLA Modules:
  0.0 246.9 jit_solution(15073609402460015227)
XLA Ops:
  0.7 0.7 stack.57
  1.4 0.7 stack.58
  2.0 0.1 pad.30.clone
  2.1 0.1 fusion.5
  2.2 0.6 copy.51
  2.8 4.5 %copy.46 = bf16[768,2304]{0,1:T(8,128)(2,1)S(1)} copy(bf16[768,2304]{1,0:T(8,128)(2,1)} %w_ref.1) | data formatting | bytes 7077888 | tf_op args[9]
  7.3 0.0 copy-start.2
  7.3 0.1 constant_dynamic-slice_fusion
  7.4 0.0 copy-start.5
  7.4 0.0 copy-start.10
  7.5 0.1 pad.13
  7.5 1.5 copy.47.own_w_ref
  9.1 0.8 fusion.19
  9.8 0.7 add_convert_fusion
  10.5 0.1 pad.34.clone
  10.6 0.7 maximum_maximum_fusion.mine_ref
  11.3 0.6 pad.12.table_ref
  11.9 12.8 %gather.1 = (f32[4,24,512]{2,1,0:T(8,128)}, f32[8,16,128]{2,1,0:T(8,128)}) custom-call(f32[24,512]{1,0:T(8,128)} %maximum_maximum_fusion.mine_ref, f32[16,128]{1,0:T(8,128)} %pad.12.table_ref), custom_call_target="tpu_custom_call" | custom-call | tf_op jit(solution)/shard_map/gather/pallas_call | solution.py:118
  24.8 0.6 stack.59.vec_ref
  25.4 17.8 %embed.1 = (bf16[2048,768]{1,0:T(8,128)(2,1)}, bf16[768,2048]{1,0:T(8,128)(2,1)}, bf16[2048,768]{1,0:T(8,128)(2,1)}, bf16[2048,768]{1,0:T(8,128)(2,1)}, bf16[4,4...) custom-call(s32[1]{0:T(128)} %bitcast.5.z_ref, ...), custom_call_target="tpu_custom_call" | custom-call | tf_op jit(solution)/shard_map/embed/pallas_call | solution.py:369
  43.4 0.6 pad_maximum_fusion.2.vec_ref
  44.0 0.6 reshape.114.b1_ref
  44.6 62.0 %layer.1 = (f32[512,768]{1,0:T(8,128)}, f32[512,768]{1,0:T(8,128)}, bf16[4,512,256]{2,1,0:T(8,128)(2,1)}, bf16[768,768]{1,0:T(8,128)(2,1)}, bf16[768,3072]{1,0:T...) custom-call(f32[4,24,512]{2,1,0:T(8,128)} %get-tuple-element.50.tok_ref, ...), custom_call_target="tpu_custom_call" | custom-call | tf_op jit(solution)/shard_map/layer/pallas_call | solution.py:537
  106.6 86.8 %attention_back_scatter.1 = (bf16[2048,768]{1,0:T(8,128)(2,1)}, f32[96,768]{1,0:T(8,128)}, f32[24,3072]{1,0:T(8,128)}, f32[24,768]{1,0:T(8,128)}) custom-call(f32[4,24,512]{2,1,0:T(8,128)} %get-tuple-element.50.tok_ref, bf16[2048,768]{1,0:T(8,128)(2,1)} %get-tuple-element.57.own_ref, bf16[4,512,256]{2,1,0:T(8,128)(2,1)} %get-tuple-element.58.msg_ref, ...), custom_call_target="tpu_custom_call" | custom-call | tf_op jit(solution)/shard_map/attention_back_scatter/pallas_call | solution.py:774
  193.4 15.2 %embed_back.1 = (bf16[768,768]{1,0:T(8,128)(2,1)}, f32[4,16,512]{2,1,0:T(8,128)}, f32[16,1024]{1,0:T(8,128)}, f32[24,768]{1,0:T(8,128)}) custom-call(s32[1]{0:T(128)} %bitcast.5.z_ref, f32[4,24,512]{2,1,0:T(8,128)} %get-tuple-element.50.tok_ref, bf16[2048,768]{1,0:T(8,128)(2,1)} %get-tuple-element.62.grad_ref, ...), custom_call_target="tpu_custom_call" | custom-call | tf_op jit(solution)/shard_map/embed_back/pallas_call | solution.py:883
  208.7 0.8 fusion.22
  209.5 0.1 broadcast_multiply_fusion
  209.6 0.9 pad_maximum_fusion.1
  210.5 0.9 copy_bitcast_fusion
  211.4 0.7 pad_maximum_fusion.small_ref
  212.1 22.5 %tail.1 = (f32[4,24,768]{2,1,0:T(8,128)}, f32[8,8,384]{2,1,0:T(8,128)}, f32[8,256]{1,0:T(8,128)}, f32[16,512]{1,0:T(8,128)}) custom-call(bf16[2,2,2,96,768]{4,3,2,1,0:T(8,128)(2,1)} %bitcast.53, f32[8,8,640]{2,1,0:T(8,128)} %pad_maximum_fusion.small_ref, f32[4,16,512]{2,1,0:T(8,128)} %get-tuple-element.73.noise_ref), custom_call_target="tpu_custom_call" | custom-call | tf_op jit(solution)/shard_map/tail/pallas_call | solution.py:978
  234.7 0.8 slice_bitcast_fusion.1
  235.5 0.7 squeeze.37
  236.2 0.7 squeeze.38
  236.9 0.6 reshape.126
  237.5 1.1 reshape.124
  238.6 0.1 slice_bitcast_fusion
  238.7 0.2 copy.50
  238.9 0.9 reshape_reshape.3
  239.8 0.7 fusion.12
  240.4 0.6 fusion
  241.0 0.5 slice.120
  241.6 1.3 fusion.3
  242.8 1.2 slice.116
  244.0 0.6 copy.57
  244.6 0.6 copy.58
  245.3 0.7 copy.59
  246.0 0.7 copy.60
  (46 shorter events, 0.2 us)
Async XLA Ops:
  7.3 4.0 %copy-start.2 = (f32[104,16]{0,1:T(8,128)S(1)}, f32[104,16]{0,1:T(8,128)}, u32[]{:S(2)}) copy-start(f32[104,16]{0,1:T(8,128)} %param.25) | copy-start | bytes 19972
  7.4 3.2 %copy-start.5 = (f32[512,16]{0,1:T(8,128)S(1)}, f32[512,16]{0,1:T(8,128)}, u32[]{:S(2)}) copy-start(f32[512,16]{0,1:T(8,128)} %param.24) | copy-start | bytes 98308
  7.4 17.3 %copy-start.9 = (f32[768]{0:T(1024)S(1)}, f32[768]{0:T(1024)}, u32[]{:S(2)}) copy-start(f32[768]{0:T(1024)} %param.27) | copy-start | bytes 9220
  7.4 17.3 %copy-start.10 = (f32[768]{0:T(1024)S(1)}, f32[768]{0:T(1024)}, u32[]{:S(2)}) copy-start(f32[768]{0:T(1024)} %param.28) | copy-start | bytes 9220
  7.4 17.3 %copy-start.11 = (f32[768]{0:T(1024)S(1)}, f32[768]{0:T(1024)}, u32[]{:S(2)}) copy-start(f32[768]{0:T(1024)} %param.29) | copy-start | bytes 9220
  9.0 34.2 %copy-start.12 = (f32[768]{0:T(1024)S(1)}, f32[768]{0:T(1024)}, u32[]{:S(2)}) copy-start(f32[768]{0:T(1024)} %param.34) | copy-start | bytes 9220
  9.0 34.3 %copy-start.13 = (f32[768]{0:T(1024)S(1)}, f32[768]{0:T(1024)}, u32[]{:S(2)}) copy-start(f32[768]{0:T(1024)} %param.35) | copy-start | bytes 9220
  9.0 34.3 %copy-start.14 = (f32[768]{0:T(1024)S(1)}, f32[768]{0:T(1024)}, u32[]{:S(2)}) copy-start(f32[768]{0:T(1024)} %param.36) | copy-start | bytes 9220
  9.0 34.3 %copy-start.15 = (f32[768]{0:T(1024)S(1)}, f32[768]{0:T(1024)}, u32[]{:S(2)}) copy-start(f32[768]{0:T(1024)} %param.40) | copy-start | bytes 9220
  9.1 34.9 %copy-start.7 = (f32[3072]{0:T(1024)S(1)}, f32[3072]{0:T(1024)}, u32[]{:S(2)}) copy-start(f32[3072]{0:T(1024)} %param.38) | copy-start | bytes 36868
  193.4 16.2 %copy-start.6 = (f32[8,768]{1,0:T(8,128)S(1)}, f32[8,768]{1,0:T(8,128)}, u32[]{:S(2)}) copy-start(f32[8,768]{1,0:T(8,128)} %get-tuple-element.70) | copy-start | bytes 73732
  208.6 36.0 %copy-start.3 = (f32[24,768]{1,0:T(8,128)S(1)}, f32[24,768]{1,0:T(8,128)}, u32[]{:S(2)}) copy-start(f32[24,768]{1,0:T(8,128)} %get-tuple-element.127) | copy-start | bytes 221188
  208.7 36.6 %copy-start.1 = (f32[24,3072]{1,0:T(8,128)S(1)}, f32[24,3072]{1,0:T(8,128)}, u32[]{:S(2)}) copy-start(f32[24,3072]{1,0:T(8,128)} %get-tuple-element.131) | copy-start | bytes 884740
  210.5 35.5 %copy-start = (f32[96,768]{1,0:T(8,128)S(1)}, f32[96,768]{1,0:T(8,128)}, u32[]{:S(2)}) copy-start(f32[96,768]{1,0:T(8,128)} %get-tuple-element.133) | copy-start | bytes 884740
  234.7 6.9 %copy-start.8 = (f32[8,256]{1,0:T(8,128)S(1)}, f32[8,256]{1,0:T(8,128)}, u32[]{:S(2)}) copy-start(f32[8,256]{1,0:T(8,128)} %get-tuple-element.75) | copy-start | bytes 24580
  234.7 9.4 %copy-start.4 = (f32[16,512]{1,0:T(8,128)S(1)}, f32[16,512]{1,0:T(8,128)}, u32[]{:S(2)}) copy-start(f32[16,512]{1,0:T(8,128)} %get-tuple-element.74) | copy-start | bytes 98308
